TPU v7x, 512 devices: a whole 4x8x8 slice. The times are simulated.
512 devices in a mesh: grp: 8 (over z_hi, x), gx: 8 (over z_lo, core), gy: 8 (over y).
Axes of the slice: x: 4, y: 8, z: 8 (z_hi: 2, z_lo: 4; z = z_hi * 4 + z_lo), core: 2. Of those that a mesh axis runs over, the one named last changes fastest.
Arguments:
- efield: float32 [8, 3, 128, 128, 128], P('grp', None, 'gx', 'gy'), may hold values from -6 to 6
- hfield: float32 [8, 3, 128, 128, 128], P('grp', None, 'gx', 'gy'), may hold values from -6 to 6
- fwd_dft: bfloat16 [8, 2, 2, 3, 128, 128, 128], P('grp', None, None, None, 'gx', 'gy'), may hold values from -6 to 6
- adj_dft: bfloat16 [8, 2, 2, 3, 128, 128, 128], P('grp', None, None, None, 'gx', 'gy'), may hold values from -6 to 6
- permittivity: float32 [128, 128, 128], P('gx', 'gy'), may hold values from 1 to 4
- source_amp: float32 [8, 128, 128], P('grp', 'gx', 'gy'), may hold values from -6 to 6
- source_plane: int32 [8], P('grp'), may hold values from 4 to 123
- freqs: float32 [8, 2], P('grp'), may hold values from 0.2 to 1.5
- pml_width: int32 [2], replicated, may hold values from 2 to 7
- design_blocks: int32 [128], replicated, may hold values from 0 to 255, as said below
Outputs:
- grad_step: float32 [2, 128, 128, 128], P(None, 'gx', 'gy')
Inputs may be any that keep to these rules, and one draw needn't show every extreme that they name: `design_blocks`: distinct block numbers.
All inputs are finite; a program needn't handle non-finite values.
Results may differ from a plain program's by a relative error of at most 0.0003.
Values sent between devices are 32-bit elements; how exact they have to be, the bound alone decides.
A program may use at most 64 MiB of HBM per device.

v0:
```python
import jax
import jax.numpy as jnp
from jax import lax
from jax.sharding import PartitionSpec as P

BS = 8
STEPS = 2
courant = 0.5
absorb = 0.8


def shifted(value, axis, steps):
    count = lax.axis_size(axis)
    leading, last = (max(0, -steps), min(count, count - steps))
    return lax.ppermute(value, axis, [(source, source + steps) for source in range(leading, last)])


def ahead_z(field):
    zero = jnp.zeros_like(field[:, :, :1])
    return jnp.concatenate([field[:, :, 1:], zero], 2) - field


def behind_z(field):
    zero = jnp.zeros_like(field[:, :, :1])
    return field - jnp.concatenate([zero, field[:, :, :-1]], 2)


def profile(cells, count, width):
    place = cells.astype(jnp.float32)
    dist = jnp.minimum(place, count - 1.0 - place)
    wide = width.astype(jnp.float32)
    return jnp.maximum(0.0, (wide - dist) / wide) ** 2


def update_magnetic(fields_e, fields_h, damp):
    ex, ey, ez = fields_e
    hx, hy, hz = fields_h
    rim_x = shifted(jnp.stack([ey[0], ez[0]]), "gx", -1)
    rim_y = shifted(jnp.stack([ex[:, 0], ez[:, 0]]), "gy", -1)
    ey_dx = jnp.concatenate([ey[1:], rim_x[0][None]], 0) - ey
    ez_dx = jnp.concatenate([ez[1:], rim_x[1][None]], 0) - ez
    ex_dy = jnp.concatenate([ex[:, 1:], rim_y[0][:, None]], 1) - ex
    ez_dy = jnp.concatenate([ez[:, 1:], rim_y[1][:, None]], 1) - ez
    hx = damp * (hx - courant * (ez_dy - ahead_z(ey)))
    hy = damp * (hy - courant * (ahead_z(ex) - ez_dx))
    hz = damp * (hz - courant * (ey_dx - ex_dy))
    return (hx, hy, hz)


def update_electric(fields_e, fields_h, damp, coef, drive):
    ex, ey, ez = fields_e
    hx, hy, hz = fields_h
    last_x = hx.shape[0] - 1
    last_y = hx.shape[1] - 1
    rim_x = shifted(jnp.stack([hy[last_x], hz[last_x]]), "gx", 1)
    rim_y = shifted(jnp.stack([hx[:, last_y], hz[:, last_y]]), "gy", 1)
    hy_dx = hy - jnp.concatenate([rim_x[0][None], hy[:-1]], 0)
    hz_dx = hz - jnp.concatenate([rim_x[1][None], hz[:-1]], 0)
    hx_dy = hx - jnp.concatenate([rim_y[0][:, None], hx[:, :-1]], 1)
    hz_dy = hz - jnp.concatenate([rim_y[1][:, None], hz[:, :-1]], 1)
    ex = damp * (ex + coef * (hz_dy - behind_z(hy)))
    ey = damp * (ey + coef * (behind_z(hx) - hz_dx))
    ez = damp * (ez + coef * (hy_dx - hx_dy) + drive)
    return (ex, ey, ez)


def body(
    efield,
    hfield,
    fwd_dft,
    adj_dft,
    permittivity,
    source_amp,
    source_plane,
    freqs,
    pml_width,
    design_blocks,
):
    cells_x, cells_y, cells_z = permittivity.shape
    total_x = cells_x * lax.axis_size("gx")
    total_y = cells_y * lax.axis_size("gy")
    global_x = lax.axis_index("gx") * cells_x + jnp.arange(cells_x, dtype=jnp.int32)
    global_y = lax.axis_index("gy") * cells_y + jnp.arange(cells_y, dtype=jnp.int32)
    plane = (jnp.arange(cells_z, dtype=jnp.int32) == source_plane[0]).astype(jnp.float32)
    shaped = source_amp[0][:, :, None] * plane[None, None, :]
    omega = freqs[0]
    acc = adj_dft[0].astype(jnp.float32)
    damp = jnp.exp(
        -absorb
        * (
            profile(global_x, total_x, pml_width[0])[:, None]
            + profile(global_y, total_y, pml_width[1])[None, :]
        )
    )[:, :, None]
    coef = courant / permittivity
    fields_e = (efield[0, 0], efield[0, 1], efield[0, 2])
    fields_h = (hfield[0, 0], hfield[0, 1], hfield[0, 2])
    for step in range(STEPS):
        tval = jnp.float32(step + 1)
        fields_h = update_magnetic(fields_e, fields_h, damp)
        fields_e = update_electric(
            fields_e, fields_h, damp, coef, shaped * jnp.sin(omega[0] * tval)
        )
        efull = jnp.stack(fields_e)
        cosv = jnp.cos(omega * tval)[:, None, None, None, None]
        sinv = jnp.sin(omega * tval)[:, None, None, None, None]
        acc = jnp.stack([acc[:, 0] + cosv * efull, acc[:, 1] - sinv * efull], axis=1)
    cell_id = (global_x // BS)[:, None] * (total_y // BS) + (global_y // BS)[None, :]
    mask = jnp.any(design_blocks[:, None, None] == cell_id[None], axis=0).astype(jnp.float32)[
        :, :, None
    ]
    term = jnp.sum(fwd_dft[0].astype(jnp.float32) * acc, axis=(1, 2)) * mask[None]
    count = jnp.float32(design_blocks.shape[0] * BS * BS * cells_z)
    grad = lax.psum(term, "grp")
    squares = lax.psum(jnp.sum(grad * grad, axis=(1, 2, 3)), ("gx", "gy"))
    return grad / jnp.sqrt(squares / count + 1e-05)[:, None, None, None]


def solution(mesh):
    in_specs = (
        P("grp", None, "gx", "gy", None),
        P("grp", None, "gx", "gy", None),
        P("grp", None, None, None, "gx", "gy", None),
        P("grp", None, None, None, "gx", "gy", None),
        P("gx", "gy", None),
        P("grp", "gx", "gy"),
        P("grp"),
        P("grp", None),
        P(),
        P(),
    )
    out_specs = P(None, "gx", "gy", None)
    return jax.shard_map(body, mesh=mesh, in_specs=in_specs, out_specs=out_specs, check_vma=False)
```

profile of v0, /device:TPU:8, one launch (start us, length us, event | category | flops | bytes accessed | tf_op | source)
XLA Modules:
  0.0 310.4 jit_solution(465055666218704547)
XLA Ops:
  6.5 1.1 slice_bitcast_fusion.1
  7.7 7.7 %collective-permute-start.1 = (f32[2,16,128]{2,1,0:T(8,128)S(1)}, f32[2,16,128]{2,1,0:T(8,128)S(1)}, u32[]{:S(2)}, u32[]{:S(2)}) collective-permute-start(f32[2,16,128]{2,1,0:T(8,128)S(1)} %pad_maximum_fusion.3), channel_id=1, source_target_pairs={{1,0},{2,1},{3,2},{4,3},{5,4},{6,5},{7,6},{9,8},{10,9},{11,10},{12... | collective-permute-start | bytes 49160 | tf_op jit(solution)/shard_map/ppermute | solution.py:15
  15.5 0.7 slice_bitcast_fusion.6
  16.2 1.3 collective-permute-start
  17.5 1.0 slice_bitcast_fusion.4
  18.5 1.4 fusion.73
  21.9 0.7 cosine_bitcast_fusion.1
  22.6 0.1 bitcast_convert_fusion
  23.0 0.4 compare_reduce_fusion
  24.0 0.1 fusion.15
  24.3 3.0 collective-permute-start.3
  27.4 1.9 collective-permute-start.2
  29.4 3.7 %collective-permute-done.2 = f32[2,16,128]{2,1,0:T(8,128)S(1)} collective-permute-done((f32[2,16,128]{2,1,0:T(8,128)S(1)}, f32[2,16,128]{2,1,0:T(8,128)S(1)}, u32[]{:S(2)}, u32[]{:S(2)}) %collective-permute-start.2) | collective-permute-done | bytes 16416 | tf_op jit(solution)/shard_map/ppermute | solution.py:15
  33.0 0.2 fusion.19
  33.3 0.1 fusion.27
  33.5 1.3 collective-permute-start.4
  35.1 1.9 collective-permute-start.5
  37.0 3.7 %collective-permute-done.5 = f32[2,16,128]{2,1,0:T(8,128)S(1)} collective-permute-done((f32[2,16,128]{2,1,0:T(8,128)S(1)}, f32[2,16,128]{2,1,0:T(8,128)S(1)}, u32[]{:S(2)}, u32[]{:S(2)}) %collective-permute-start.5) | collective-permute-done | bytes 16416 | tf_op jit(solution)/shard_map/ppermute | solution.py:15
  40.7 0.2 fusion.38
  41.0 2.0 collective-permute-start.7
  43.1 1.9 collective-permute-start.6
  45.0 0.1 fusion.52
  45.2 3.6 %collective-permute-done.6 = f32[2,16,128]{2,1,0:T(8,128)S(1)} collective-permute-done((f32[2,16,128]{2,1,0:T(8,128)S(1)}, f32[2,16,128]{2,1,0:T(8,128)S(1)}, u32[]{:S(2)}, u32[]{:S(2)}) %collective-permute-start.6) | collective-permute-done | bytes 16416 | tf_op jit(solution)/shard_map/ppermute | solution.py:15
  48.7 0.2 fusion.43
  49.0 0.3 fusion.2
  49.3 0.8 copy-done.3
  50.1 0.2 fusion
  50.3 0.8 broadcast_multiply_fusion
  51.1 115.3 %all-reduce.10.cloned.1.call-done = f32[2,16,16,128]{3,2,1,0:T(8,128)} async-done(((f32[2,16,16,128]{3,2,1,0:T(8,128)}), f32[2,16,16,128]{3,2,1,0:T(8,128)}) %all-reduce.10.cloned.1.call-update) | async-done | bytes 262160 | tf_op jit(solution)/shard_map/psum | solution.py:114
  166.4 1.1 multiply_reduce_fusion
  167.5 134.2 %psum.15 = f32[2]{0:T(128)S(1)} all-reduce(f32[2]{0:T(128)S(1)} %multiply_reduce_fusion), channel_id=1, replica_groups=mesh['grp'=8,'gx'=8,'gy'=8] {'gx','gy'}, use_global_device_ids=true, to_apply=%region_4.5 | all-reduce | flops 2 | bytes 16 | tf_op jit(solution)/shard_map/psum | solution.py:115
  301.8 1.7 broadcast_divide_fusion
  (76 shorter events, 1.1 us)
Async XLA Ops:
  6.5 16.0 %copy-start.2 = (bf16[1,2,2,3,16,16,128]{6,5,4,3,2,1,0:T(8,128)(2,1)S(1)}, bf16[1,2,2,3,16,16,128]{6,5,4,3,2,1,0:T(8,128)(2,1)}, u32[]{:S(2)}) copy-start(bf16[1,2,2,3,16,16,128]{6,5,4,3,2,1,0:T(8,128)(2,1)} %param.13) | copy-start | bytes 2359300
  6.5 159.9 %all-reduce.10.cloned.1.call-start = ((), (), s32[]{:S(2)}) async-start(), calls=%async_computation | async-start | bytes 524288 | tf_op jit(solution)/shard_map/psum | solution.py:114
  7.7 15.3 %copy-start.7 = (s32[128]{0:T(128)S(1)}, s32[128]{0:T(128)}, u32[]{:S(2)}) copy-start(s32[128]{0:T(128)} %param.19) | copy-start | bytes 1540
  7.7 16.2 %collective-permute-start.1 = (f32[2,16,128]{2,1,0:T(8,128)S(1)}, f32[2,16,128]{2,1,0:T(8,128)S(1)}, u32[]{:S(2)}, u32[]{:S(2)}) collective-permute-start(f32[2,16,128]{2,1,0:T(8,128)S(1)} %pad_maximum_fusion.3), channel_id=1, source_target_pairs={{1,0},{2,1},{3,2},{4,3},{5,4},{6,5},{7,6},{9,8},{10,9},{11,10},{12... | collective-permute-start | bytes 49160 | tf_op jit(solution)/shard_map/ppermute | solution.py:15
  16.2 7.8 %collective-permute-start = (f32[2,16,128]{2,1,0:T(8,128)S(1)}, f32[2,16,128]{2,1,0:T(8,128)S(1)}, u32[]{:S(2)}, u32[]{:S(2)}) collective-permute-start(f32[2,16,128]{2,1,0:T(8,128)S(1)} %pad_maximum_fusion.2), channel_id=1, source_target_pairs={{8,0},{16,8},{24,16},{32,24},{40,32},{48,40},{56,48},{9,1},{17,9},... | collective-permute-start | bytes 49160 | tf_op jit(solution)/shard_map/ppermute | solution.py:15
  22.6 1.1 copy-start.6
  22.6 1.4 copy-start
  22.6 1.4 copy-start.4
  23.7 9.4 %copy-start.1 = (f32[16,16,128]{2,1,0:T(8,128)S(1)}, f32[16,16,128]{2,1,0:T(8,128)}, u32[]{:S(2)}) copy-start(f32[16,16,128]{2,1,0:T(8,128)} %param.14) | copy-start | bytes 393220
  23.7 9.4 %copy-start.5 = (f32[1,16,16]{2,1,0:T(8,128)S(1)}, f32[1,16,16]{2,1,0:T(8,128)}, u32[]{:S(2)}) copy-start(f32[1,16,16]{2,1,0:T(8,128)} %param.15) | copy-start | bytes 3076
  24.3 5.0 %collective-permute-start.3 = (f32[2,16,128]{2,1,0:T(8,128)S(1)}, f32[2,16,128]{2,1,0:T(8,128)S(1)}, u32[]{:S(2)}, u32[]{:S(2)}) collective-permute-start(f32[2,16,128]{2,1,0:T(8,128)S(1)} %pad_maximum_fusion.5), channel_id=1, source_target_pairs={{0,8},{8,16},{16,24},{24,32},{32,40},{40,48},{48,56},{1,9},{9,17},... | collective-permute-start | bytes 49160 | tf_op jit(solution)/shard_map/ppermute | solution.py:15
  27.4 5.6 %collective-permute-start.2 = (f32[2,16,128]{2,1,0:T(8,128)S(1)}, f32[2,16,128]{2,1,0:T(8,128)S(1)}, u32[]{:S(2)}, u32[]{:S(2)}) collective-permute-start(f32[2,16,128]{2,1,0:T(8,128)S(1)} %pad_maximum_fusion.4), channel_id=1, source_target_pairs={{0,1},{1,2},{2,3},{3,4},{4,5},{5,6},{6,7},{8,9},{9,10},{10,11},{11... | collective-permute-start | bytes 49160 | tf_op jit(solution)/shard_map/ppermute | solution.py:15
  33.5 3.6 %collective-permute-start.4 = (f32[2,16,128]{2,1,0:T(8,128)S(1)}, f32[2,16,128]{2,1,0:T(8,128)S(1)}, u32[]{:S(2)}, u32[]{:S(2)}) collective-permute-start(f32[2,16,128]{2,1,0:T(8,128)S(1)} %pad_maximum_fusion.6), channel_id=1, source_target_pairs={{8,0},{16,8},{24,16},{32,24},{40,32},{48,40},{56,48},{9,1},{17,9},... | collective-permute-start | bytes 49160 | tf_op jit(solution)/shard_map/ppermute | solution.py:15
  35.1 5.6 %collective-permute-start.5 = (f32[2,16,128]{2,1,0:T(8,128)S(1)}, f32[2,16,128]{2,1,0:T(8,128)S(1)}, u32[]{:S(2)}, u32[]{:S(2)}) collective-permute-start(f32[2,16,128]{2,1,0:T(8,128)S(1)} %pad_maximum_fusion.7), channel_id=1, source_target_pairs={{1,0},{2,1},{3,2},{4,3},{5,4},{6,5},{7,6},{9,8},{10,9},{11,10},{12... | collective-permute-start | bytes 49160 | tf_op jit(solution)/shard_map/ppermute | solution.py:15
  41.0 4.0 %collective-permute-start.7 = (f32[2,16,128]{2,1,0:T(8,128)S(1)}, f32[2,16,128]{2,1,0:T(8,128)S(1)}, u32[]{:S(2)}, u32[]{:S(2)}) collective-permute-start(f32[2,16,128]{2,1,0:T(8,128)S(1)} %pad_maximum_fusion.9), channel_id=1, source_target_pairs={{0,8},{8,16},{16,24},{24,32},{32,40},{40,48},{48,56},{1,9},{9,17},... | collective-permute-start | bytes 49160 | tf_op jit(solution)/shard_map/ppermute | solution.py:15
  43.1 5.7 %collective-permute-start.6 = (f32[2,16,128]{2,1,0:T(8,128)S(1)}, f32[2,16,128]{2,1,0:T(8,128)S(1)}, u32[]{:S(2)}, u32[]{:S(2)}) collective-permute-start(f32[2,16,128]{2,1,0:T(8,128)S(1)} %pad_maximum_fusion.8), channel_id=1, source_target_pairs={{0,1},{1,2},{2,3},{3,4},{4,5},{5,6},{6,7},{8,9},{9,10},{10,11},{11... | collective-permute-start | bytes 49160 | tf_op jit(solution)/shard_map/ppermute | solution.py:15
  49.0 1.1 copy-start.3
Sparse Core Ops, SparseCore 0:
  51.3 115.1 all-reduce.9
where the time goes:
time: 311 us; the launch traced here: 310 us
  blocking collectives  134 us (43%)
  waiting for transfers between devices  126 us (41%)
  starting transfers between devices  21.1 us (7%)
  between operations  16.2 us (5%)
  other arithmetic  6.79 us (2%)
  local copies, waits for them, and re-layouts  5.7 us (2%)
    psum x1, blocking collectives, body(): squares = lax.psum(jnp.sum(grad * grad, axis=(1, 2, 3)), ('gx', 'gy'))  134 us
    psum x1, waiting for transfers between devices, body(): grad = lax.psum(term, 'grp')  115 us
    ppermute x8, starting transfers between devices, shifted(): lax.ppermute(value, axis, [(source, source + steps) for source in range(l...  21.1 us
    ppermute x8, waiting for transfers between devices, shifted(): lax.ppermute(value, axis, [(source, source + steps) for source in range(l...  11 us
  transfers between devices with their start and end apart: 9, of which 4 were waited for; matrix products, arithmetic and copies ran while one was open for 2% of the time, Pallas kernels for 0%

commit v1 on v0

--- a/solution.py
+++ b/solution.py
@@ -112,7 +112,7 @@
     term = jnp.sum(fwd_dft[0].astype(jnp.float32) * acc, axis=(1, 2)) * mask[None]
     count = jnp.float32(design_blocks.shape[0] * BS * BS * cells_z)
     grad = lax.psum(term, "grp")
-    squares = lax.psum(jnp.sum(grad * grad, axis=(1, 2, 3)), ("gx", "gy"))
+    squares = lax.psum(lax.psum(jnp.sum(grad * grad, axis=(1, 2, 3)), "gy"), "gx")
     return grad / jnp.sqrt(squares / count + 1e-05)[:, None, None, None]
 
 

time: 311 us -> 208 us (0.67)
  the two profiles are of different devices: /device:TPU:8 before, /device:TPU:1 now
where the time goes in v1:
time: 208 us
  waiting for transfers between devices  116 us (56%)
  blocking collectives  36.1 us (17%)
  starting transfers between devices  27.3 us (13%)
  between operations  16.1 us (8%)
  other arithmetic  6.78 us (3%)
  local copies, waits for them, and re-layouts  5.65 us (3%)
    psum x1, waiting for transfers between devices, body(): grad = lax.psum(term, 'grp')  110 us
    ppermute x8, starting transfers between devices, shifted(): lax.ppermute(value, axis, [(source, source + steps) for source in range(l...  27.3 us
    psum x1, blocking collectives, body(): lax.psum(lax.psum(jnp.sum(grad * grad, axis=(1, 2, 3)), 'gy'), 'gx')  22.9 us
    psum x1, blocking collectives, body(): lax.psum(jnp.sum(grad * grad, axis=(1, 2, 3)), 'gy')  13.2 us
    ppermute x8, waiting for transfers between devices, shifted(): lax.ppermute(value, axis, [(source, source + steps) for source in range(l...  5.27 us
  transfers between devices with their start and end apart: 9, of which 5 were waited for; matrix products, arithmetic and copies ran while one was open for 3% of the time, Pallas kernels for 0%

profile of v1, /device:TPU:1, one launch (start us, length us, event | category | flops | bytes accessed | tf_op | source)
XLA Modules:
  0.0 207.5 jit_solution(2682592217169148444)
XLA Ops:
  6.5 1.1 slice_bitcast_fusion.1
  7.7 1.3 collective-permute-start.1
  9.0 0.7 slice_bitcast_fusion.6
  9.8 8.8 %collective-permute-start = (f32[2,16,128]{2,1,0:T(8,128)S(1)}, f32[2,16,128]{2,1,0:T(8,128)S(1)}, u32[]{:S(2)}, u32[]{:S(2)}) collective-permute-start(f32[2,16,128]{2,1,0:T(8,128)S(1)} %pad_maximum_fusion.2), channel_id=1, source_target_pairs={{8,0},{16,8},{24,16},{32,24},{40,32},{48,40},{56,48},{9,1},{17,9},... | collective-permute-start | bytes 49160 | tf_op jit(solution)/shard_map/ppermute | solution.py:15
  18.5 1.0 slice_bitcast_fusion.4
  19.5 1.3 fusion.73
  22.8 0.7 cosine_bitcast_fusion.1
  23.6 0.1 bitcast_convert_fusion
  23.9 0.4 compare_reduce_fusion
  24.9 0.1 fusion.15
  25.2 1.9 collective-permute-start.3
  27.2 4.3 %collective-permute-start.2 = (f32[2,16,128]{2,1,0:T(8,128)S(1)}, f32[2,16,128]{2,1,0:T(8,128)S(1)}, u32[]{:S(2)}, u32[]{:S(2)}) collective-permute-start(f32[2,16,128]{2,1,0:T(8,128)S(1)} %pad_maximum_fusion.4), channel_id=1, source_target_pairs={{0,1},{1,2},{2,3},{3,4},{4,5},{5,6},{6,7},{8,9},{9,10},{10,11},{11... | collective-permute-start | bytes 49160 | tf_op jit(solution)/shard_map/ppermute | solution.py:15
  31.5 0.8 collective-permute-done.2
  32.4 0.2 fusion.19
  32.8 3.3 %collective-permute-start.4 = (f32[2,16,128]{2,1,0:T(8,128)S(1)}, f32[2,16,128]{2,1,0:T(8,128)S(1)}, u32[]{:S(2)}, u32[]{:S(2)}) collective-permute-start(f32[2,16,128]{2,1,0:T(8,128)S(1)} %pad_maximum_fusion.6), channel_id=1, source_target_pairs={{8,0},{16,8},{24,16},{32,24},{40,32},{48,40},{56,48},{9,1},{17,9},... | collective-permute-start | bytes 49160 | tf_op jit(solution)/shard_map/ppermute | solution.py:15
  36.4 1.3 collective-permute-start.5
  37.7 0.2 collective-permute-done.4
  37.8 3.6 %collective-permute-done.5 = f32[2,16,128]{2,1,0:T(8,128)S(1)} collective-permute-done((f32[2,16,128]{2,1,0:T(8,128)S(1)}, f32[2,16,128]{2,1,0:T(8,128)S(1)}, u32[]{:S(2)}, u32[]{:S(2)}) %collective-permute-start.5) | collective-permute-done | bytes 16416 | tf_op jit(solution)/shard_map/ppermute | solution.py:15
  41.4 0.2 fusion.38
  41.7 2.9 %collective-permute-start.7 = (f32[2,16,128]{2,1,0:T(8,128)S(1)}, f32[2,16,128]{2,1,0:T(8,128)S(1)}, u32[]{:S(2)}, u32[]{:S(2)}) collective-permute-start(f32[2,16,128]{2,1,0:T(8,128)S(1)} %pad_maximum_fusion.9), channel_id=1, source_target_pairs={{0,8},{8,16},{16,24},{24,32},{32,40},{40,48},{48,56},{1,9},{9,17},... | collective-permute-start | bytes 49160 | tf_op jit(solution)/shard_map/ppermute | solution.py:15
  44.6 3.6 %collective-permute-start.6 = (f32[2,16,128]{2,1,0:T(8,128)S(1)}, f32[2,16,128]{2,1,0:T(8,128)S(1)}, u32[]{:S(2)}, u32[]{:S(2)}) collective-permute-start(f32[2,16,128]{2,1,0:T(8,128)S(1)} %pad_maximum_fusion.8), channel_id=1, source_target_pairs={{0,1},{1,2},{2,3},{3,4},{4,5},{5,6},{6,7},{8,9},{9,10},{10,11},{11... | collective-permute-start | bytes 49160 | tf_op jit(solution)/shard_map/ppermute | solution.py:15
  48.4 0.7 collective-permute-done.6
  49.1 0.2 fusion.43
  49.4 0.3 fusion.2
  49.6 0.8 copy-done.3
  50.5 0.2 fusion
  50.7 0.8 broadcast_multiply_fusion
  51.5 110.3 %all-reduce.10.cloned.1.call-done = f32[2,16,16,128]{3,2,1,0:T(8,128)} async-done(((f32[2,16,16,128]{3,2,1,0:T(8,128)}), f32[2,16,16,128]{3,2,1,0:T(8,128)}) %all-reduce.10.cloned.1.call-update) | async-done | bytes 262160 | tf_op jit(solution)/shard_map/psum | solution.py:114
  161.8 1.1 multiply_reduce_fusion
  162.8 13.2 %psum.22 = f32[2]{0:T(128)S(1)} all-reduce(f32[2]{0:T(128)S(1)} %multiply_reduce_fusion), channel_id=1, replica_groups=mesh['grp'=8,'gx'=8,'gy'=8] {'gy'}, use_global_device_ids=true, to_apply=%region_4.5 | all-reduce | flops 2 | bytes 16 | tf_op jit(solution)/shard_map/psum | solution.py:115
  176.1 22.9 %psum.23 = f32[2]{0:T(128)S(1)} all-reduce(f32[2]{0:T(128)S(1)} %psum.22), channel_id=1, replica_groups=mesh['grp'=8,'gx'=8,'gy'=8] {'gx'}, use_global_device_ids=true, to_apply=%region_5.6 | all-reduce | flops 2 | bytes 16 | tf_op jit(solution)/shard_map/psum | solution.py:115
  198.9 1.7 broadcast_divide_fusion
  (77 shorter events, 1.3 us)
Async XLA Ops:
  6.5 17.0 %copy-start.2 = (bf16[1,2,2,3,16,16,128]{6,5,4,3,2,1,0:T(8,128)(2,1)S(1)}, bf16[1,2,2,3,16,16,128]{6,5,4,3,2,1,0:T(8,128)(2,1)}, u32[]{:S(2)}) copy-start(bf16[1,2,2,3,16,16,128]{6,5,4,3,2,1,0:T(8,128)(2,1)} %param.13) | copy-start | bytes 2359300
  6.5 155.2 %all-reduce.10.cloned.1.call-start = ((), (), s32[]{:S(2)}) async-start(), calls=%async_computation | async-start | bytes 524288 | tf_op jit(solution)/shard_map/psum | solution.py:114
  7.7 16.2 %copy-start.7 = (s32[128]{0:T(128)S(1)}, s32[128]{0:T(128)}, u32[]{:S(2)}) copy-start(s32[128]{0:T(128)} %param.19) | copy-start | bytes 1540
  7.7 17.1 %collective-permute-start.1 = (f32[2,16,128]{2,1,0:T(8,128)S(1)}, f32[2,16,128]{2,1,0:T(8,128)S(1)}, u32[]{:S(2)}, u32[]{:S(2)}) collective-permute-start(f32[2,16,128]{2,1,0:T(8,128)S(1)} %pad_maximum_fusion.3), channel_id=1, source_target_pairs={{1,0},{2,1},{3,2},{4,3},{5,4},{6,5},{7,6},{9,8},{10,9},{11,10},{12... | collective-permute-start | bytes 49160 | tf_op jit(solution)/shard_map/ppermute | solution.py:15
  9.8 15.1 %collective-permute-start = (f32[2,16,128]{2,1,0:T(8,128)S(1)}, f32[2,16,128]{2,1,0:T(8,128)S(1)}, u32[]{:S(2)}, u32[]{:S(2)}) collective-permute-start(f32[2,16,128]{2,1,0:T(8,128)S(1)} %pad_maximum_fusion.2), channel_id=1, source_target_pairs={{8,0},{16,8},{24,16},{32,24},{40,32},{48,40},{56,48},{9,1},{17,9},... | collective-permute-start | bytes 49160 | tf_op jit(solution)/shard_map/ppermute | solution.py:15
  23.5 1.1 copy-start.6
  23.5 1.4 copy-start
  23.5 1.4 copy-start.4
  24.6 7.8 %copy-start.1 = (f32[16,16,128]{2,1,0:T(8,128)S(1)}, f32[16,16,128]{2,1,0:T(8,128)}, u32[]{:S(2)}) copy-start(f32[16,16,128]{2,1,0:T(8,128)} %param.14) | copy-start | bytes 393220
  24.6 7.8 %copy-start.5 = (f32[1,16,16]{2,1,0:T(8,128)S(1)}, f32[1,16,16]{2,1,0:T(8,128)}, u32[]{:S(2)}) copy-start(f32[1,16,16]{2,1,0:T(8,128)} %param.15) | copy-start | bytes 3076
  25.2 6.3 %collective-permute-start.3 = (f32[2,16,128]{2,1,0:T(8,128)S(1)}, f32[2,16,128]{2,1,0:T(8,128)S(1)}, u32[]{:S(2)}, u32[]{:S(2)}) collective-permute-start(f32[2,16,128]{2,1,0:T(8,128)S(1)} %pad_maximum_fusion.5), channel_id=1, source_target_pairs={{0,8},{8,16},{16,24},{24,32},{32,40},{40,48},{48,56},{1,9},{9,17},... | collective-permute-start | bytes 49160 | tf_op jit(solution)/shard_map/ppermute | solution.py:15
  27.2 5.1 %collective-permute-start.2 = (f32[2,16,128]{2,1,0:T(8,128)S(1)}, f32[2,16,128]{2,1,0:T(8,128)S(1)}, u32[]{:S(2)}, u32[]{:S(2)}) collective-permute-start(f32[2,16,128]{2,1,0:T(8,128)S(1)} %pad_maximum_fusion.4), channel_id=1, source_target_pairs={{0,1},{1,2},{2,3},{3,4},{4,5},{5,6},{6,7},{8,9},{9,10},{10,11},{11... | collective-permute-start | bytes 49160 | tf_op jit(solution)/shard_map/ppermute | solution.py:15
  32.8 5.1 %collective-permute-start.4 = (f32[2,16,128]{2,1,0:T(8,128)S(1)}, f32[2,16,128]{2,1,0:T(8,128)S(1)}, u32[]{:S(2)}, u32[]{:S(2)}) collective-permute-start(f32[2,16,128]{2,1,0:T(8,128)S(1)} %pad_maximum_fusion.6), channel_id=1, source_target_pairs={{8,0},{16,8},{24,16},{32,24},{40,32},{48,40},{56,48},{9,1},{17,9},... | collective-permute-start | bytes 49160 | tf_op jit(solution)/shard_map/ppermute | solution.py:15
  36.4 5.1 %collective-permute-start.5 = (f32[2,16,128]{2,1,0:T(8,128)S(1)}, f32[2,16,128]{2,1,0:T(8,128)S(1)}, u32[]{:S(2)}, u32[]{:S(2)}) collective-permute-start(f32[2,16,128]{2,1,0:T(8,128)S(1)} %pad_maximum_fusion.7), channel_id=1, source_target_pairs={{1,0},{2,1},{3,2},{4,3},{5,4},{6,5},{7,6},{9,8},{10,9},{11,10},{12... | collective-permute-start | bytes 49160 | tf_op jit(solution)/shard_map/ppermute | solution.py:15
  41.7 6.6 %collective-permute-start.7 = (f32[2,16,128]{2,1,0:T(8,128)S(1)}, f32[2,16,128]{2,1,0:T(8,128)S(1)}, u32[]{:S(2)}, u32[]{:S(2)}) collective-permute-start(f32[2,16,128]{2,1,0:T(8,128)S(1)} %pad_maximum_fusion.9), channel_id=1, source_target_pairs={{0,8},{8,16},{16,24},{24,32},{32,40},{40,48},{48,56},{1,9},{9,17},... | collective-permute-start | bytes 49160 | tf_op jit(solution)/shard_map/ppermute | solution.py:15
  44.6 4.5 %collective-permute-start.6 = (f32[2,16,128]{2,1,0:T(8,128)S(1)}, f32[2,16,128]{2,1,0:T(8,128)S(1)}, u32[]{:S(2)}, u32[]{:S(2)}) collective-permute-start(f32[2,16,128]{2,1,0:T(8,128)S(1)} %pad_maximum_fusion.8), channel_id=1, source_target_pairs={{0,1},{1,2},{2,3},{3,4},{4,5},{5,6},{6,7},{8,9},{9,10},{10,11},{11... | collective-permute-start | bytes 49160 | tf_op jit(solution)/shard_map/ppermute | solution.py:15
  49.3 1.1 copy-start.3
Sparse Core Ops, SparseCore 0:
  51.6 110.0 all-reduce.9
